TPU v7x, 128 devices: a whole 4x4x4 slice. The times are simulated.
128 devices in a mesh: dp: 8 (over z, core), tensor: 16 (over x, y).
Axes of the slice: x: 4, y: 4, z: 4, core: 2. Of those that a mesh axis runs over, the one named last changes fastest.
Arguments:
- tokens: bfloat16 [4096, 4096], P('dp', 'tensor'), may hold values from -10 to 10
- out_grad: bfloat16 [4096, 4096], P('dp', 'tensor'), may hold values from -10 to 10
- gate_weight: bfloat16 [4096, 12288], P(None, 'tensor'), may hold values from -0.09375 to 0.09375
- up_weight: bfloat16 [4096, 12288], P(None, 'tensor'), may hold values from -0.09375 to 0.09375
- down_weight: bfloat16 [12288, 4096], P('tensor'), may hold values from -0.0546875 to 0.0546875
- slot_ffn_block: int32 [768], P('tensor'), may hold values from 0 to 5
- slot_model_block: int32 [768], P('tensor'), may hold values from 0 to 31
- slot_kind: int32 [768], P('tensor'), may hold values from 0 to 2
- live_count: int32 [16], P('tensor'), may hold values from 1 to 48, as said below
Outputs:
- input_grad: bfloat16 [4096, 4096], P('dp', 'tensor')
- block_grads: float32 [768, 128, 128], P('tensor', 'dp')
Inputs may be any that keep to these rules, and one draw needn't show every extreme that they name: Slots of holder h are 0 to live_count[h] - 1 in its 48 slots; some holder uses all 48.
All inputs are finite; a program needn't handle non-finite values.
Results may differ from a plain program's by a relative error of at most 0.019.
Values may be sent and summed in bfloat16 or wider, within the bound.
A program may use at most 128 MiB of HBM per device.

v0:
```python
import math

import jax
import jax.numpy as jnp
from jax import lax
from jax.sharding import PartitionSpec as P

TILE = 128
LEN = 128


def per_device(
    tokens,
    out_grad,
    gate_weight,
    up_weight,
    down_weight,
    slot_ffn_block,
    slot_model_block,
    slot_kind,
    live_count,
):
    x_full, g_full = (
        lax.all_gather(tokens, "tensor", axis=1, tiled=True),
        lax.all_gather(out_grad, "tensor", axis=1, tiled=True),
    )
    tok_rows = x_full.shape[0]
    model_width = x_full.shape[1]
    ffn_local = gate_weight.shape[1]
    tensor_size = lax.axis_size("tensor")
    slot_cap = slot_kind.shape[0]
    gate_pre = jnp.dot(x_full, gate_weight, preferred_element_type=jnp.float32)
    up_proj = jnp.dot(x_full, up_weight, preferred_element_type=jnp.float32)
    sigmoid_gate = jax.nn.sigmoid(gate_pre)
    hidden = (gate_pre * sigmoid_gate * up_proj).astype(jnp.bfloat16)
    hidden_grad = lax.dot_general(
        g_full, down_weight, (((1,), (1,)), ((), ())), preferred_element_type=jnp.float32
    )
    grad_gate = (
        hidden_grad * up_proj * sigmoid_gate * (1.0 + gate_pre * (1.0 - sigmoid_gate))
    ).astype(jnp.bfloat16)
    grad_up = (hidden_grad * gate_pre * sigmoid_gate).astype(jnp.bfloat16)
    partial_sum = lax.dot_general(
        grad_gate, gate_weight, (((1,), (1,)), ((), ())), preferred_element_type=jnp.float32
    ) + lax.dot_general(
        grad_up, up_weight, (((1,), (1,)), ((), ())), preferred_element_type=jnp.float32
    )
    input_grad = lax.psum_scatter(
        partial_sum.astype(jnp.bfloat16), "tensor", scatter_dimension=1, tiled=True
    )
    live_slot = (jnp.arange(slot_cap, dtype=jnp.int32) < live_count[0]).astype(jnp.float32)
    x_cols = jnp.take(x_full.reshape(tok_rows, model_width // TILE, TILE), slot_model_block, axis=1)
    g_cols = jnp.take(g_full.reshape(tok_rows, model_width // TILE, TILE), slot_model_block, axis=1)
    h_cols = jnp.take(hidden.reshape(tok_rows, ffn_local // TILE, TILE), slot_ffn_block, axis=1)
    gg_cols = jnp.take(grad_gate.reshape(tok_rows, ffn_local // TILE, TILE), slot_ffn_block, axis=1)
    gu_cols = jnp.take(grad_up.reshape(tok_rows, ffn_local // TILE, TILE), slot_ffn_block, axis=1)
    kinds = slot_kind[None, :, None]
    left_cols = jnp.where(kinds == 2, h_cols, x_cols).reshape(tok_rows // LEN, LEN, slot_cap, TILE)
    right_cols = jnp.where(kinds == 0, gg_cols, jnp.where(kinds == 1, gu_cols, g_cols)).reshape(
        tok_rows // LEN, LEN, slot_cap, TILE
    )
    block_tiles = jnp.einsum(
        "slci,slcj->scij", left_cols, right_cols, preferred_element_type=jnp.float32
    )
    block_tiles = block_tiles * live_slot[None, :, None, None]
    square_local = jnp.sum(block_tiles * block_tiles, axis=(1, 2, 3))
    norm_total = lax.psum(square_local, "tensor")
    bound = 0.33 * TILE * math.sqrt(LEN * slot_cap * tensor_size)
    clip = jnp.minimum(1.0, bound / jnp.sqrt(norm_total + 1e-06))
    local_sum = jnp.sum(clip[:, None, None, None] * block_tiles, axis=0)
    block_grads = lax.psum_scatter(
        local_sum.astype(jnp.bfloat16), "dp", scatter_dimension=1, tiled=True
    ).astype(jnp.float32)
    return (input_grad, block_grads)


def solution(mesh):
    return jax.shard_map(
        per_device,
        mesh=mesh,
        in_specs=(
            P("dp", "tensor"),
            P("dp", "tensor"),
            P(None, "tensor"),
            P(None, "tensor"),
            P("tensor", None),
            P("tensor"),
            P("tensor"),
            P("tensor"),
            P("tensor"),
        ),
        out_specs=(P("dp", "tensor"), P("tensor", "dp", None)),
        check_vma=False,
    )
```

profile of v0, /device:TPU:0, one launch (start us, length us, event | category | flops | bytes accessed | tf_op | source)
XLA Modules:
  0.0 358.0 jit_solution(3972378992437677433)
XLA Ops:
  7.2 1.8 copy.22
  9.1 1.8 copy.21
  12.9 0.7 compare_and_fusion
  14.3 50.3 %all-gather.5.cloned.1.call-done = bf16[512,4096]{0,1:T(8,128)(2,1)} async-done(((bf16[512,256]{0,1:T(8,128)(2,1)}), bf16[512,4096]{0,1:T(8,128)(2,1)}) %all-gather.5.cloned.1.call-update) | async-done | bytes 4194320 | tf_op jit(solution)/shard_map/all_gather | solution.py:24
  64.6 6.5 %copy.25 = bf16[512,32,128]{2,0,1:T(8,128)(2,1)} copy(bf16[512,32,128]{0,2,1:T(8,128)(2,1)} %bitcast.33) | data formatting | bytes 8388608 | tf_op jit(solution)/shard_map/reshape | solution.py:52
  71.1 8.7 %fusion.5 = f32[512,768]{1,0:T(8,128)} fusion(bf16[512,4096]{0,1:T(8,128)(2,1)} %all-gather.5.cloned.1.call-done, bf16[4096,768]{1,0:T(8,128)(2,1)} %param.15), kind=kOutput, calls=%fused_computation.30 | convolution fusion | flops 3221225472 | bytes 12058624 | tf_op jit(solution)/shard_map/dot_general | solution.py:32
  79.8 38.7 %all-gather.3.cloned.1.call-done = bf16[512,4096]{0,1:T(8,128)(2,1)} async-done(((bf16[512,256]{0,1:T(8,128)(2,1)}), bf16[512,4096]{0,1:T(8,128)(2,1)}) %all-gather.3.cloned.1.call-update) | async-done | bytes 4194320 | tf_op jit(solution)/shard_map/all_gather | solution.py:25
  118.5 7.3 %fusion.4 = f32[512,768]{1,0:T(8,128)S(1)} fusion(bf16[512,4096]{0,1:T(8,128)(2,1)} %all-gather.3.cloned.1.call-done, bf16[768,4096]{1,0:T(8,128)(2,1)} %param.17), kind=kOutput, calls=%fused_computation.29 | convolution fusion | flops 3221225472 | bytes 12058624 | tf_op jit(solution)/shard_map/dot_general | solution.py:36
  125.8 7.8 %multiply_convert_fusion = (bf16[512,768]{1,0:T(8,128)(2,1)S(1)}, bf16[512,768]{1,0:T(8,128)(2,1)}, bf16[512,768]{1,0:T(8,128)(2,1)S(1)}) fusion(f32[512,768]{1,0:T(8,128)S(1)} %copy-done.5, f32[512,768]{1,0:T(8,128)S(1)} %fusion.4, bf16[512,4096]{0,1:T(8,128)(2,1)S(1)} %copy-done, bf16[4096,768]{1,0:T(8,128)(2,1)} %param.16), kind=kOutput, calls=%fused_computation.14 | convolution fusion | flops 3227516928 | bytes 15990784 | tf_op jit(solution)/shard_map/dot_general | solution.py:33
  134.2 6.5 %copy.31 = bf16[512,32,128]{2,0,1:T(8,128)(2,1)} copy(bf16[512,32,128]{0,2,1:T(8,128)(2,1)} %bitcast.34) | data formatting | bytes 8388608 | tf_op jit(solution)/shard_map/reshape | solution.py:53
  140.7 7.1 %gather_fusion.1 = bf16[48,512,128]{2,1,0:T(8,128)(2,1)} fusion(bf16[512,32,128]{2,0,1:T(8,128)(2,1)} %copy.25, s32[1024]{0:T(1024)S(1)} %pad_clamp_fusion), kind=kCustom, calls=%fused_computation.1.clone | custom fusion | bytes 12583104 | tf_op jit(solution)/shard_map/jit(_take)/gather | solution.py:52
  147.8 7.2 %gather_fusion.4 = bf16[48,512,128]{2,1,0:T(8,128)(2,1)} fusion(bf16[512,32,128]{2,0,1:T(8,128)(2,1)} %copy.31, s32[1024]{0:T(1024)S(1)} %pad_clamp_fusion), kind=kCustom, calls=%fused_computation.4.clone | custom fusion | bytes 12583104 | tf_op jit(solution)/shard_map/jit(_take)/gather | solution.py:53
  155.6 4.9 %gather_fusion = bf16[48,512,128]{2,1,0:T(8,128)(2,1)} fusion(bf16[512,6,128]{2,0,1:T(8,128)(2,1)S(1)} %copy.24, s32[1024]{0:T(1024)S(1)} %pad_clamp_fusion.1), kind=kCustom, calls=%fused_computation.clone | custom fusion | bytes 12583104 | tf_op jit(solution)/shard_map/jit(_take)/gather | solution.py:54
  160.5 4.8 %gather_fusion.3 = bf16[48,512,128]{2,1,0:T(8,128)(2,1)} fusion(bf16[512,6,128]{2,0,1:T(8,128)(2,1)S(1)} %copy.30, s32[1024]{0:T(1024)S(1)} %pad_clamp_fusion.1), kind=kCustom, calls=%fused_computation.3.clone | custom fusion | bytes 12583104 | tf_op jit(solution)/shard_map/jit(_take)/gather | solution.py:56
  166.0 4.9 %gather_fusion.2 = bf16[48,512,128]{2,1,0:T(8,128)(2,1)} fusion(bf16[512,6,128]{2,0,1:T(8,128)(2,1)S(1)} %copy.28, s32[1024]{0:T(1024)S(1)} %pad_clamp_fusion.1), kind=kCustom, calls=%fused_computation.2.clone | custom fusion | bytes 12583104 | tf_op jit(solution)/shard_map/jit(_take)/gather | solution.py:55
  171.0 14.0 %bitcast_select_fusion.1 = (bf16[512,48,128]{2,0,1:T(8,128)(2,1)S(1)}, bf16[512,48,128]{2,0,1:T(8,128)(2,1)}) fusion(bf16[48,512,128]{2,1,0:T(8,128)(2,1)} %gather_fusion.1, bf16[48,512,128]{2,1,0:T(8,128)(2,1)} %gather_fusion, pred[48]{0:T(512)(128)(4,1)S(1)} %get-tuple-element.14, pred[48]{0:T(512)(128)(4,1)S(1)} %get-tuple-element.15, ...), kind=kLoop, calls=%fused_computation.13 | loop fusion | flops 25165824 | bytes 44040432 | tf_op jit(solution)/shard_map/jit(_where)/select_n | solution.py:58
  185.0 10.4 %multiply_reduce_fusion.1 = (f32[4]{0:T(128)S(1)}, f32[4,48,128,128]{3,2,1,0:T(8,128)}) fusion(f32[48]{0:T(128)S(1)} %compare_convert_fusion, bf16[4,128,48,128]{3,1,0,2:T(8,128)(2,1)} %bitcast.32, bf16[4,128,48,128]{3,1,0,2:T(8,128)(2,1)S(1)} %bitcast.31), kind=kOutput, calls=%fused_computation.6 | convolution fusion | flops 814743552 | bytes 25166032 | tf_op jit(solution)/shard_map/slci,slcj->scij/dot_general | solution.py:62
  195.4 38.5 %psum.7 = f32[4]{0:T(128)S(1)} all-reduce(f32[4]{0:T(128)S(1)} %get-tuple-element.12), channel_id=1, replica_groups=mesh['dp'=8,'tensor'=16] {'tensor'}, use_global_device_ids=true, to_apply=%region_2.0 | all-reduce | flops 4 | bytes 32 | tf_op jit(solution)/shard_map/psum | solution.py:67
  233.9 8.1 %multiply_reduce_fusion = bf16[48,128,128]{2,1,0:T(8,128)(2,1)} fusion(f32[4,48,128,128]{3,2,1,0:T(8,128)} %get-tuple-element.13, f32[4]{0:T(128)S(1)} %multiply_minimum_fusion, f32[48]{0:T(128)S(1)} %compare_convert_fusion), kind=kLoop, calls=%fused_computation.5 | loop fusion | flops 8650752 | bytes 14155984 | tf_op jit(solution)/shard_map/reduce_sum | solution.py:70
  242.1 5.8 %fusion.6 = f32[512,4096]{1,0:T(8,128)S(1)} fusion(bf16[512,768]{1,0:T(8,128)(2,1)S(1)} %copy-done.4, bf16[4096,768]{1,0:T(8,128)(2,1)} %param.15), kind=kOutput, calls=%fused_computation.31 | convolution fusion | flops 3221225472 | bytes 15466496 | tf_op jit(solution)/shard_map/dot_general | solution.py:43
  247.9 7.9 %add_convert_fusion = bf16[512,4096]{1,0:T(8,128)(2,1)} fusion(f32[512,4096]{1,0:T(8,128)S(1)} %fusion.6, bf16[512,768]{1,0:T(8,128)(2,1)S(1)} %copy-done.2, bf16[4096,768]{1,0:T(8,128)(2,1)} %param.16), kind=kOutput, calls=%fused_computation.7 | convolution fusion | flops 3225419776 | bytes 19660800 | tf_op jit(solution)/shard_map/dot_general | solution.py:45
  255.8 15.7 %reduce-scatter.5.cloned.1.call-done = bf16[48,16,128]{2,1,0:T(8,128)(2,1)} async-done(((bf16[48,128,128]{2,1,0:T(8,128)(2,1)}), bf16[48,16,128]{2,1,0:T(8,128)(2,1)}) %reduce-scatter.5.cloned.1.call-update) | async-done | bytes 196624 | tf_op jit(solution)/shard_map/reduce_scatter | solution.py:71
  271.5 1.7 convert_element_type.31
  273.2 78.3 %reduce-scatter.3.cloned.1.call-done = bf16[512,256]{1,0:T(8,128)(2,1)} async-done(((bf16[512,4096]{1,0:T(8,128)(2,1)}), bf16[512,256]{1,0:T(8,128)(2,1)}) %reduce-scatter.3.cloned.1.call-update) | async-done | bytes 262160 | tf_op jit(solution)/shard_map/reduce_scatter | solution.py:48
  (33 shorter events, 4.2 us)
Async XLA Ops:
  7.2 57.4 %all-gather.5.cloned.1.call-start = ((), (), s32[]{:S(2)}) async-start(), calls=%async_computation.3 | async-start | bytes 4456448 | tf_op jit(solution)/shard_map/all_gather | solution.py:24
  9.0 109.4 %all-gather.3.cloned.1.call-start = ((), (), s32[]{:S(2)}) async-start(), calls=%async_computation.2 | async-start | bytes 4456448 | tf_op jit(solution)/shard_map/all_gather | solution.py:25
  10.9 260.6 %reduce-scatter.5.cloned.1.call-start = ((), (), s32[]{:S(2)}) async-start(), calls=%async_computation.5 | async-start | bytes 1769472 | tf_op jit(solution)/shard_map/reduce_scatter | solution.py:71
  118.5 7.3 %copy-start = (bf16[512,4096]{0,1:T(8,128)(2,1)S(1)}, bf16[512,4096]{0,1:T(8,128)(2,1)}, u32[]{:S(2)}) copy-start(bf16[512,4096]{0,1:T(8,128)(2,1)} %all-gather.5.cloned.1.call-done) | copy-start | bytes 12582916
  118.5 7.3 %copy-start.5 = (f32[512,768]{1,0:T(8,128)S(1)}, f32[512,768]{1,0:T(8,128)}, u32[]{:S(2)}) copy-start(f32[512,768]{1,0:T(8,128)} %fusion.5) | copy-start | bytes 4718596
  133.6 21.4 %copy-start.1 = (bf16[512,768]{1,0:T(8,128)(2,1)}, bf16[512,768]{1,0:T(8,128)(2,1)S(1)}, u32[]{:S(2)}) copy-start(bf16[512,768]{1,0:T(8,128)(2,1)S(1)} %get-tuple-element.6) | copy-start | bytes 2359300
  160.5 4.9 %copy-start.3 = (bf16[512,768]{1,0:T(8,128)(2,1)S(1)}, bf16[512,768]{1,0:T(8,128)(2,1)}, u32[]{:S(2)}) copy-start(bf16[512,768]{1,0:T(8,128)(2,1)} %get-tuple-element.5) | copy-start | bytes 2359300
  233.9 8.2 %copy-start.4 = (bf16[512,768]{1,0:T(8,128)(2,1)S(1)}, bf16[512,768]{1,0:T(8,128)(2,1)}, u32[]{:S(2)}) copy-start(bf16[512,768]{1,0:T(8,128)(2,1)} %get-tuple-element.5) | copy-start | bytes 2359300
  242.0 5.9 %copy-start.2 = (bf16[512,768]{1,0:T(8,128)(2,1)S(1)}, bf16[512,768]{1,0:T(8,128)(2,1)}, u32[]{:S(2)}) copy-start(bf16[512,768]{1,0:T(8,128)(2,1)} %copy-done.1) | copy-start | bytes 2359300
  242.0 109.4 %reduce-scatter.3.cloned.1.call-start = ((), (), s32[]{:S(2)}) async-start(), calls=%async_computation.4 | async-start | bytes 4456448 | tf_op jit(solution)/shard_map/reduce_scatter | solution.py:48
Sparse Core Ops, SparseCore 0:
  10.7 53.8 all-gather.4
  67.3 51.0 all-gather.2
  242.1 29.3 reduce-scatter.4
  275.3 76.1 reduce-scatter.2
where the time goes:
time: 359 us; the launch traced here: 358 us
  waiting for transfers between devices  183 us (51%)
  matrix products  47.9 us (13%)
  local copies, waits for them, and re-layouts  47.4 us (13%)
  blocking collectives  38.5 us (11%)
  other arithmetic  26.5 us (7%)
  between operations  14.5 us (4%)
    reduce_scatter x1, waiting for transfers between devices, per_device(): lax.psum_scatter(partial_sum.astype(jnp.bfloat16), 'tensor', scatter_dime...  78.3 us
    all_gather x1, waiting for transfers between devices, per_device(): lax.all_gather(tokens, 'tensor', axis=1, tiled=True)  50.3 us
    all_gather x1, waiting for transfers between devices, per_device(): lax.all_gather(out_grad, 'tensor', axis=1, tiled=True)  38.7 us
    psum x1, blocking collectives, per_device(): norm_total = lax.psum(square_local, 'tensor')  38.5 us
    reduce_scatter x1, waiting for transfers between devices, per_device(): lax.psum_scatter(local_sum.astype(jnp.bfloat16), 'dp', scatter_dimension=...  15.7 us
    select_n x1, other arithmetic, per_device(): jnp.where(kinds == 2, h_cols, x_cols)  14 us
    dot_general x1, matrix products, per_device(): jnp.einsum('slci,slcj->scij', left_cols, right_cols, preferred_element_ty...  10.4 us
    dot_general x1, matrix products, per_device(): gate_pre = jnp.dot(x_full, gate_weight, preferred_element_type=jnp.float32)  8.71 us
  transfers between devices with their start and end apart: 4, of which 4 were waited for; matrix products, arithmetic and copies ran while one was open for 10% of the time, Pallas kernels for 0%

commit v1 on v0

v1 whole, which is shorter than its diff:
```python
import math

import jax
import jax.numpy as jnp
from jax import lax
from jax.experimental import pallas as pl
from jax.experimental.pallas import tpu as pltpu
from jax.sharding import PartitionSpec as P

TILE = 128
LEN = 128
ROWS = 256
SLOTS = 48
NX = 4
XB, GB, HB, GGB, GUB = 0, 32, 64, 70, 76
BLOCKS = 82
OFF = (0, -1, 1, 2)
OFF2 = (2, 1, -1, 0)
MESH = pl.DeviceIdType.MESH
BOUND = 0.33 * TILE * math.sqrt(LEN * 768)
NT = (((1,), (1,)), ((), ()))
TN = (((0,), (0,)), ((), ()))
DPG = 3
DPS = SLOTS // DPG


def mod4(v):
    return lax.rem(v + 8, 4)


def kernel(
    tok,
    og,
    gw,
    uw,
    dw,
    sf,
    sm,
    sk,
    lc,
    out_x,
    out_b,
    cat0,
    cat1,
    wg,
    wu,
    wd,
    acc_g,
    acc_u,
    acc_h,
    p0,
    p1,
    r1,
    r2,
    r3,
    r4,
    tiles,
    nr,
    ssum,
    cr,
    zs,
    zr,
    own_sem,
    w_sem,
    ag_s,
    ag_r,
    rs_s,
    rs_r,
    nr_s,
    nr_r,
    c_s,
    c_r,
    z_s,
    z_r,
):
    dp = lax.axis_index("dp")
    me = lax.axis_index("tensor")
    cx, cy = me // 4, lax.rem(me, 4)
    cz, cc = dp // 2, lax.rem(dp, 2)
    cats = (cat0, cat1)
    ps = (p0, p1)
    sends = []

    own = []
    for h in range(2):
        for arr, src in ((0, tok), (1, og)):
            for k in range(2):
                c = pltpu.make_async_copy(
                    src.at[pl.ds(h * ROWS, ROWS), pl.ds(k * TILE, TILE)],
                    cats[h].at[32 * arr + 2 * me + k],
                    own_sem.at[h, arr, k],
                )
                c.start()
                own.append(c)
    wcopies = [
        pltpu.make_async_copy(gw, wg, w_sem.at[0]),
        pltpu.make_async_copy(uw, wu, w_sem.at[1]),
    ] + [
        pltpu.make_async_copy(dw.at[:, pl.ds(1024 * i, 1024)], wd.at[i], w_sem.at[2 + i])
        for i in range(4)
    ]
    for c in wcopies:
        c.start()

    barrier = pltpu.get_barrier_semaphore()
    for k in range(1, 16):
        pl.semaphore_signal(
            barrier, inc=1, device_id=(dp, lax.rem(me + k, 16)), device_id_type=MESH
        )
    pl.semaphore_signal(barrier, inc=1, device_id=(cz * 2 + 1 - cc, me), device_id_type=MESH)
    for k in range(1, 4):
        pl.semaphore_signal(
            barrier, inc=1, device_id=(mod4(cz + k) * 2 + cc, me), device_id_type=MESH
        )
    pl.semaphore_wait(barrier, 19)

    def rcopy(src, dst, ssem, rsem, dev):
        return pltpu.make_async_remote_copy(
            src_ref=src, dst_ref=dst, send_sem=ssem, recv_sem=rsem, device_id=dev, device_id_type=MESH
        )

    def send(src, dst, ssem, rsem, dev):
        c = rcopy(src, dst, ssem, rsem, dev)
        c.start()
        sends.append(c)

    def tensor_at(first_is_x, a1, a2):
        return a1 * 4 + a2 if first_is_x else a2 * 4 + a1

    def ag(h, arr):
        fx = arr == 0
        c1, c2 = (cx, cy) if fx else (cy, cx)

        def dev(d1, d2):
            return (dp, tensor_at(fx, mod4(c1 + d1), mod4(c2 + d2)))

        def region(d1, d2, part):
            t = tensor_at(fx, mod4(c1 + d1), mod4(c2 + d2))
            rows = (pl.ds(0, ROWS), pl.ds(0, ROWS // 2), pl.ds(ROWS // 2, ROWS // 2))[part]
            return cats[h].at[pl.ds(32 * arr + 2 * t, 2), rows, :]

        def put(idx, d1, d2, part, e1, e2):
            r = region(d1, d2, part)
            send(r, r, ag_s.at[h, arr, idx], ag_r.at[h, arr, idx], dev(e1, e2))

        def got(idx, d1, d2, part):
            r = region(d1, d2, part)
            rcopy(r, r, ag_s.at[h, arr, idx], ag_r.at[h, arr, idx], dev(1, 0)).wait_recv()

        def start():
            put(0, 0, 0, 0, 1, 0)
            put(1, 0, 0, 0, -1, 0)
            put(4, 0, 0, 0, 0, 1)
            put(5, 0, 0, 0, 0, -1)

        def spread(j):
            put(4 + 4 * j, OFF[j], 0, 0, 0, 1)
            put(5 + 4 * j, OFF[j], 0, 0, 0, -1)

        def e1():
            got(0, -1, 0, 0)
            put(2, -1, 0, 1, 1, 0)
            spread(1)

        def e2():
            got(1, 1, 0, 0)
            put(3, 1, 0, 2, -1, 0)
            spread(2)

        def e3():
            got(2, 2, 0, 1)
            got(3, 2, 0, 2)
            spread(3)

        def e4(j):
            got(4 + 4 * j, OFF[j], -1, 0)
            put(6 + 4 * j, OFF[j], -1, 1, 0, 1)
            got(5 + 4 * j, OFF[j], 1, 0)
            put(7 + 4 * j, OFF[j], 1, 2, 0, -1)

        def e5(j):
            got(6 + 4 * j, OFF[j], 2, 1)
            got(7 + 4 * j, OFF[j], 2, 2)

        return start, e1, e2, e3, e4, e5

    AG = [[ag(h, arr) for arr in range(2)] for h in range(2)]

    def ag_step(h, k, *a):
        for arr in range(2):
            AG[h][arr][k](*a)

    def fwd(h, off):
        cat = cats[h]
        yy, xx = mod4(cy + off), mod4(cx + off)

        def body(n, _):
            cols = pl.ds(pl.multiple_of(n * 256, 256), 256)
            lhs = jnp.concatenate(
                [cat[2 * (4 * i + yy) + k] for i in range(4) for k in range(2)], axis=1
            )
            for w, acc in ((wg, acc_g), (wu, acc_u)):
                rhs = jnp.concatenate([w[4 * i + yy, :, cols] for i in range(4)], axis=0)
                v = jnp.dot(lhs, rhs, preferred_element_type=jnp.float32)
                for k in range(2):
                    vk = v[:, k * TILE : (k + 1) * TILE]
                    acc[2 * n + k] = vk if off == 0 else acc[2 * n + k] + vk
            lhs = jnp.concatenate([cat[GB + 8 * xx + k] for k in range(8)], axis=1)
            v = lax.dot_general(lhs, wd[xx, cols, :], NT, preferred_element_type=jnp.float32)
            for k in range(2):
                vk = v[:, k * TILE : (k + 1) * TILE]
                acc_h[2 * n + k] = vk if off == 0 else acc_h[2 * n + k] + vk
            return 0

        lax.fori_loop(0, 3, body, 0)

    def pointwise(h):
        cat = cats[h]

        def body(f, _):
            for r in range(4):
                rows = pl.ds(r * 64, 64)
                g, u, hg = acc_g[f, rows, :], acc_u[f, rows, :], acc_h[f, rows, :]
                s = 1.0 / (1.0 + jnp.exp(-g))
                gs = g * s
                cat[HB + f, rows, :] = (gs * u).astype(jnp.bfloat16)
                cat[GGB + f, rows, :] = (hg * u * s * (1.0 + g * (1.0 - s))).astype(jnp.bfloat16)
                cat[GUB + f, rows, :] = (hg * gs).astype(jnp.bfloat16)
            return 0

        lax.fori_loop(0, 6, body, 0)

    def partial(h, t):
        cat = cats[h]
        lhs = jnp.concatenate([cat[GGB + k] for k in range(12)], axis=1)
        rhs = jnp.concatenate([wg[t], wu[t]], axis=1)
        v = lax.dot_general(lhs, rhs, NT, preferred_element_type=jnp.float32)
        ps[h][t] = v.astype(jnp.bfloat16)

    def partial_y(h):
        def body(i, _):
            partial(h, mod4(cx + 2 - i) * 4 + mod4(cy + 2))
            return 0

        lax.fori_loop(0, 4, body, 0)

    def partial_x(h):
        def body(i, _):
            partial(h, mod4(cx + 2) * 4 + mod4(cy + 1 - i))
            return 0

        lax.fori_loop(0, 3, body, 0)

    def partial_rest(h):
        def body(i, _):
            partial(h, mod4(cx + 1 - lax.rem(i, 3)) * 4 + mod4(cy + 1 - i // 3))
            return 0

        lax.fori_loop(0, 9, body, 0)

    def rs(h, p):
        fx = p == 1
        c1, c2 = (cx, cy) if fx else (cy, cx)
        buf = ps[h]
        r0 = p * 128
        full, low, up = pl.ds(r0, 128), pl.ds(r0, 64), pl.ds(r0 + 64, 64)

        def dev(d1, d2):
            return (dp, tensor_at(fx, mod4(c1 + d1), mod4(c2 + d2)))

        def blk(d1, d2):
            return tensor_at(fx, mod4(c1 + d1), mod4(c2 + d2))

        def put(idx, d1, d2, rows, dst, e1, e2):
            send(buf.at[blk(d1, d2), rows, :], dst, rs_s.at[h, p, idx], rs_r.at[h, p, idx], dev(e1, e2))

        def got(idx, dst):
            rcopy(dst, dst, rs_s.at[h, p, idx], rs_r.at[h, p, idx], dev(1, 0)).wait_recv()

        def add(d1, d2, rows, *terms):
            b = blk(d1, d2)
            v = buf[b, rows, :].astype(jnp.float32)
            for ref in terms:
                v = v + ref[...].astype(jnp.float32)
            return b, v

        def addto(d1, d2, rows, *terms):
            b, v = add(d1, d2, rows, *terms)
            buf[b, rows, :] = v.astype(jnp.bfloat16)

        R1 = [[r1.at[h, p, j, k] for k in range(2)] for j in range(4)]
        R2 = [[r2.at[h, p, j, k] for k in range(2)] for j in range(4)]
        R3 = [r3.at[h, p, k] for k in range(2)]
        R4 = [r4.at[h, p, k] for k in range(2)]

        def s1(j):
            put(4 * j, 2, OFF2[j], low, R1[j][0], 1, 0)
            put(4 * j + 1, 2, OFF2[j], up, R1[j][1], -1, 0)

        def t1(j):
            got(4 * j, R1[j][0])
            addto(1, OFF2[j], low, R1[j][0])
            put(4 * j + 2, 1, OFF2[j], full, R2[j][0], 1, 0)
            got(4 * j + 1, R1[j][1])
            addto(-1, OFF2[j], up, R1[j][1])
            put(4 * j + 3, -1, OFF2[j], full, R2[j][1], -1, 0)

        def t2(j):
            got(4 * j + 2, R2[j][0])
            got(4 * j + 3, R2[j][1])
            addto(0, OFF2[j], full, R2[j][0], R2[j][1])
            if j == 0:
                put(16, 0, 2, low, R3[0], 0, 1)
                put(17, 0, 2, up, R3[1], 0, -1)

        def t3():
            got(16, R3[0])
            addto(0, 1, low, R3[0])
            put(18, 0, 1, full, R4[0], 0, 1)
            got(17, R3[1])
            addto(0, -1, up, R3[1])
            put(19, 0, -1, full, R4[1], 0, -1)

        def t4():
            got(18, R4[0])
            got(19, R4[1])
            _, v = add(0, 0, full, R4[0], R4[1])
            out_x[pl.ds(h * ROWS + r0, 128), :] = v.astype(jnp.bfloat16)

        return s1, t1, t2, t3, t4

    RS = [[rs(h, p) for p in range(2)] for h in range(2)]

    def rs_step(h, k, *a):
        for p in range(2):
            RS[h][p][k](*a)

    UN = 4

    def tiles_of(h):
        cat = cats[h]

        def body(q, carry):
            sq = list(carry)
            for i in range(UN):
                s = q * UN + i
                f, m, kd = sf[s], sm[s], sk[s]
                live = jnp.where(s < lc[0], 1.0, 0.0).astype(jnp.float32)
                li = jnp.where(kd == 2, HB + f, XB + m)
                ri = jnp.where(kd == 0, GGB + f, jnp.where(kd == 1, GUB + f, GB + m))
                for e in range(2):
                    rows = pl.ds(e * LEN, LEN)
                    v = lax.dot_general(
                        cat[li, rows, :], cat[ri, rows, :], TN, preferred_element_type=jnp.float32
                    )
                    v = v * live
                    tiles[2 * h + e, s] = v
                    sq[e] = sq[e] + jnp.sum((v * v).reshape(16, 8, TILE), axis=0)
            return tuple(sq)

        z = jnp.zeros((8, TILE), jnp.float32)
        sq = lax.fori_loop(0, SLOTS // UN, body, (z, z))
        for e in range(2):
            nr[me, pl.ds(2 * h + e, 1), :] = jnp.sum(sq[e], axis=0, keepdims=True)

    def norm_send():
        for k in range(1, 16):
            send(nr.at[me], nr.at[me], nr_s.at[k], nr_r.at[k], (dp, lax.rem(me + k, 16)))

    def norm_wait():
        for k in range(1, 16):
            src = nr.at[lax.rem(me + 16 - k, 16)]
            rcopy(src, src, nr_s.at[k], nr_r.at[k], (dp, lax.rem(me + k, 16))).wait_recv()
        tot = nr[0]
        for k in range(1, 16):
            tot = tot + nr[k]
        tot = jnp.sum(tot, axis=1, keepdims=True)
        clip = jnp.minimum(1.0, BOUND / jnp.sqrt(tot + 1e-06))
        return jnp.broadcast_to(clip, (8, TILE))

    def scaled(clip, g):
        cl = [clip[e : e + 1, :] for e in range(4)]

        def body(i, _):
            s = g * DPS + i
            v = cl[0] * tiles[0, s]
            for e in range(1, 4):
                v = v + cl[e] * tiles[e, s]
            v = v.astype(jnp.bfloat16)
            for z in range(4):
                for c in range(2):
                    ssum[z, c, s] = v[(2 * z + c) * 16 : (2 * z + c + 1) * 16, :]
            return 0

        lax.fori_loop(0, DPS, body, 0)
        sl = pl.ds(g * DPS, DPS)
        send(
            ssum.at[:, 1 - cc, sl], cr.at[:, sl], c_s.at[g], c_r.at[g], (cz * 2 + 1 - cc, me)
        )

    def core_sum(g):
        sl = pl.ds(g * DPS, DPS)
        rcopy(cr.at[:, sl], cr.at[:, sl], c_s.at[g], c_r.at[g], (cz * 2 + 1 - cc, me)).wait_recv()

        for k in range(1, 4):
            z = mod4(cz + k)
            v = ssum[z, cc, sl].astype(jnp.float32) + cr[z, sl].astype(jnp.float32)
            zs[k - 1, sl] = v.astype(jnp.bfloat16)
            send(zs.at[k - 1, sl], zr.at[k - 1, sl], z_s.at[k - 1, g], z_r.at[k - 1, g], (z * 2 + cc, me))

    def z_sum(g):
        sl = pl.ds(g * DPS, DPS)
        v = ssum[cz, cc, sl].astype(jnp.float32) + cr[cz, sl].astype(jnp.float32)
        for k in range(3):
            r = zr.at[k, sl]
            rcopy(r, r, z_s.at[k, g], z_r.at[k, g], (mod4(cz + k + 1) * 2 + cc, me)).wait_recv()
            v = v + zr[k, sl].astype(jnp.float32)
        out_b[sl] = v

    for c in own[:4]:
        c.wait()
    ag_step(0, 0)
    for c in own[4:]:
        c.wait()
    nr[me] = jnp.zeros((8, TILE), jnp.float32)
    ag_step(0, 1)
    ag_step(0, 2)
    ag_step(0, 3)
    for c in wcopies:
        c.wait()
    fwd(0, 0)
    ag_step(0, 4, 0)
    ag_step(0, 4, 1)
    ag_step(1, 0)
    ag_step(0, 4, 2)
    ag_step(0, 4, 3)
    fwd(0, -1)
    fwd(0, 1)
    ag_step(1, 1)
    ag_step(1, 2)
    for j in range(4):
        ag_step(0, 5, j)
    fwd(0, 2)
    ag_step(1, 3)
    pointwise(0)
    ag_step(1, 4, 0)
    fwd(1, 0)
    partial_y(0)
    ag_step(1, 4, 1)
    partial_x(0)
    partial_rest(0)
    ag_step(1, 4, 2)
    tiles_of(0)
    ag_step(1, 4, 3)
    for j in range(4):
        rs_step(0, 0, j)
    fwd(1, -1)
    fwd(1, 1)
    for j in range(4):
        rs_step(0, 1, j)
    for j in range(4):
        ag_step(1, 5, j)
    fwd(1, 2)
    pointwise(1)
    for j in range(4):
        rs_step(0, 2, j)
    partial_y(1)
    for j in range(4):
        RS[1][0][0](j)
    partial_x(1)
    for j in range(4):
        RS[1][1][0](j)
    rs_step(0, 3)
    tiles_of(1)
    norm_send()
    partial_rest(1)
    for j in range(4):
        rs_step(1, 1, j)
    clip = norm_wait()
    for g in range(DPG):
        scaled(clip, g)
    rs_step(0, 4)
    core_sum(0)
    for j in range(2):
        rs_step(1, 2, j)
    core_sum(1)
    for j in range(2, 4):
        rs_step(1, 2, j)
    core_sum(2)
    rs_step(1, 3)
    rs_step(1, 4)
    for g in range(DPG):
        z_sum(g)
    for c in sends:
        c.wait_send()


def per_device(
    tokens,
    out_grad,
    gate_weight,
    up_weight,
    down_weight,
    slot_ffn_block,
    slot_model_block,
    slot_kind,
    live_count,
):
    bf, f32 = jnp.bfloat16, jnp.float32
    anyspec = pl.BlockSpec(memory_space=pl.ANY)
    smem = pl.BlockSpec(memory_space=pltpu.SMEM)
    vmem = pl.BlockSpec(memory_space=pltpu.VMEM)
    dma = pltpu.SemaphoreType.DMA
    return pl.pallas_call(
        kernel,
        out_shape=(
            jax.ShapeDtypeStruct((512, 256), bf),
            jax.ShapeDtypeStruct((SLOTS, 16, TILE), f32),
        ),
        in_specs=[anyspec] * 5 + [smem] * 4,
        out_specs=(vmem, vmem),
        scratch_shapes=[
            pltpu.VMEM((BLOCKS, ROWS, TILE), bf),
            pltpu.VMEM((BLOCKS, ROWS, TILE), bf),
            pltpu.VMEM((16, 256, 768), bf),
            pltpu.VMEM((16, 256, 768), bf),
            pltpu.VMEM((4, 768, 1024), bf),
            pltpu.VMEM((6, ROWS, TILE), f32),
            pltpu.VMEM((6, ROWS, TILE), f32),
            pltpu.VMEM((6, ROWS, TILE), f32),
            pltpu.VMEM((16, ROWS, 256), bf),
            pltpu.VMEM((16, ROWS, 256), bf),
            pltpu.VMEM((2, 2, 4, 2, 64, 256), bf),
            pltpu.VMEM((2, 2, 4, 2, 128, 256), bf),
            pltpu.VMEM((2, 2, 2, 64, 256), bf),
            pltpu.VMEM((2, 2, 2, 128, 256), bf),
            pltpu.VMEM((4, SLOTS, TILE, TILE), f32),
            pltpu.VMEM((16, 8, TILE), f32),
            pltpu.VMEM((4, 2, SLOTS, 16, TILE), bf),
            pltpu.VMEM((4, SLOTS, 16, TILE), bf),
            pltpu.VMEM((3, SLOTS, 16, TILE), bf),
            pltpu.VMEM((3, SLOTS, 16, TILE), bf),
            dma((2, 2, 2)),
            dma((6,)),
            dma((2, 2, 20)),
            dma((2, 2, 20)),
            dma((2, 2, 20)),
            dma((2, 2, 20)),
            dma((16,)),
            dma((16,)),
            dma((DPG,)),
            dma((DPG,)),
            dma((3, DPG)),
            dma((3, DPG)),
        ],
        compiler_params=pltpu.CompilerParams(
            collective_id=0, has_side_effects=True, vmem_limit_bytes=62 << 20
        ),
        cost_estimate=pl.CostEstimate(
            flops=17_000_000_000, bytes_accessed=20_000_000, transcendentals=400_000
        ),
    )(
        tokens,
        out_grad,
        gate_weight.reshape(16, 256, 768),
        up_weight.reshape(16, 256, 768),
        down_weight,
        slot_ffn_block,
        slot_model_block,
        slot_kind,
        live_count,
    )


def solution(mesh):
    return jax.shard_map(
        per_device,
        mesh=mesh,
        in_specs=(
            P("dp", "tensor"),
            P("dp", "tensor"),
            P(None, "tensor"),
            P(None, "tensor"),
            P("tensor", None),
            P("tensor"),
            P("tensor"),
            P("tensor"),
            P("tensor"),
        ),
        out_specs=(P("dp", "tensor"), P("tensor", "dp", None)),
        check_vma=False,
    )
```

time: 359 us -> 105 us (0.29)
  waiting for transfers between devices: 183 us -> 0 us
  Pallas kernels: 0 us -> 98.7 us
  matrix products: 47.9 us -> 0 us
  local copies, waits for them, and re-layouts: 47.4 us -> 3.44 us
  blocking collectives: 38.5 us -> 0 us
  other arithmetic: 26.5 us -> 0 us
  between operations: 14.5 us -> 1.29 us
    pallas_call x0 -> x1, Pallas kernels: none -> 98.7 us  [per_device(): pl.pallas_call(kernel, out_shape=(jax.ShapeDtypeStruct((512, 256), bf), j...]
    reduce_scatter x2 -> x0, waiting for transfers between devices: 93.9 us -> none  [the longest x1 78.3 us: per_device(): lax.psum_scatter(partial_sum.astype(jnp.bfloat16), 'tensor', scatter_dime...]
    all_gather x2 -> x0, waiting for transfers between devices: 89 us -> none  [the longest x1 50.3 us: per_device(): lax.all_gather(tokens, 'tensor', axis=1, tiled=True)]
    dot_general x6 -> x0, matrix products: 47.9 us -> none  [the longest x1 10.4 us: per_device(): jnp.einsum('slci,slcj->scij', left_cols, right_cols, preferred_element_ty...]
    psum x1 -> x0, blocking collectives: 38.5 us -> none  [per_device(): norm_total = lax.psum(square_local, 'tensor')]
    gather x5 -> x0, local copies, waits for them, and re-layouts: 28.9 us -> none  [the longest x1 7.16 us: per_device(): jnp.take(g_full.reshape(tok_rows, model_width // TILE, TILE), slot_model_...]
    select_n x3 -> x0, other arithmetic: 15.3 us -> none  [the longest x1 14 us: per_device(): jnp.where(kinds == 2, h_cols, x_cols)]
    reshape x5 -> x0, local copies, waits for them, and re-layouts: 14 us -> none  [the longest x1 6.47 us: per_device(): g_full.reshape(tok_rows, model_width // TILE, TILE)]
  transfers between devices with their start and end apart: 4 -> 0, of which waited for: 4 -> 0; matrix products, arithmetic and copies ran while one was open for 10% -> 0% of each run, Pallas kernels for 0% -> 0%
where the time goes in v1:
time: 105 us; the launch traced here: 103 us
  Pallas kernels  98.7 us (94%)
  local copies, waits for them, and re-layouts  3.44 us (3%)
  between operations  1.29 us (1%)
    pallas_call x1, Pallas kernels, per_device(): pl.pallas_call(kernel, out_shape=(jax.ShapeDtypeStruct((512, 256), bf), j...  98.7 us
    unnamed x2, local copies, waits for them, and re-layouts  3.44 us

profile of v1, /device:TPU:0, one launch (start us, length us, event | category | flops | bytes accessed | tf_op | source)
XLA Modules:
  0.0 103.5 jit_solution(581802766544604507)
XLA Ops:
  1.3 98.7 %shard_map.104 = (bf16[512,256]{1,0:T(8,128)(2,1)}, f32[48,16,128]{2,1,0:T(8,128)}) custom-call(bf16[512,256]{1,0:T(8,128)(2,1)} %tok.1, bf16[512,256]{1,0:T(8,128)(2,1)} %og.1, bf16[16,256,768]{2,1,0:T(8,128)(2,1)} %bitcast.2, bf16[16,256,768]{2,1,0:T(8,128)(2,1)} %bitcast.3, bf16[768,4096]{1,0:T(8,128)(2,1)} %dw.1, s32[48]{0:T(128)} %sf.1, s32[48]{0:T(128)} %sm.1, ...), custom_call_target="tpu_custom_call" | custom-call | flops 16999999488 | bytes 20000000 | tf_op jit(solution)/shard_map/pallas_call | solution.py:514
  100.0 1.7 %copy.14 = bf16[512,256]{1,0:T(8,128)(2,1)} copy(bf16[512,256]{1,0:T(8,128)(2,1)} %get-tuple-element.4) | data formatting | bytes 524288
  101.7 1.8 %copy.15 = f32[48,16,128]{2,1,0:T(8,128)} copy(f32[48,16,128]{2,1,0:T(8,128)} %get-tuple-element.5) | data formatting | bytes 786432

commit v2 on v1

v2 whole, which is shorter than its diff:
```python
import math

import jax
import jax.numpy as jnp
from jax import lax
from jax.experimental import pallas as pl
from jax.experimental.pallas import tpu as pltpu
from jax.sharding import PartitionSpec as P

TILE = 128
LEN = 128
CHUNKS = (256, 256)
STARTS = tuple(sum(CHUNKS[:i]) for i in range(len(CHUNKS)))
NC = len(CHUNKS)
SEQ0 = tuple(v // LEN for v in STARTS)
NSEQ = tuple(v // LEN for v in CHUNKS)
SLOTS = 48
NX = 4
XB, GB, HB, GGB, GUB = 0, 32, 64, 70, 76
BLOCKS = 82
OFF = (0, -1, 1, 2)
OFF2 = (2, 1, -1, 0)
MESH = pl.DeviceIdType.MESH
BOUND = 0.33 * TILE * math.sqrt(LEN * 768)
NT = (((1,), (1,)), ((), ()))
TN = (((0,), (0,)), ((), ()))
NT1 = 1 + NSEQ[-1]


def mod4(v):
    return lax.rem(v + 8, 4)


def kernel(
    tok,
    og,
    gw,
    uw,
    dw,
    sf,
    sm,
    sk,
    lc,
    out_x,
    out_b,
    cats,
    wg,
    wu,
    wd,
    acc_g,
    acc_u,
    acc_h,
    ps,
    r1,
    r2,
    r3,
    r4,
    tiles,
    nr,
    xs,
    xr,
    cs,
    cr,
    zs,
    zr,
    own_sem,
    w_sem,
    ag_s,
    ag_r,
    rs_s,
    rs_r,
    nr_s,
    nr_r,
    x_s,
    x_r,
    c_s,
    c_r,
    z_s,
    z_r,
    o_sem,
    ox,
    ob,
):
    dp = lax.axis_index("dp")
    me = lax.axis_index("tensor")
    cx, cy = me // 4, lax.rem(me, 4)
    cz, cc = dp // 2, lax.rem(dp, 2)
    sends = []

    own = []
    for h in range(NC):
        for arr, src in ((0, tok), (1, og)):
            for k in range(2):
                c = pltpu.make_async_copy(
                    src.at[pl.ds(STARTS[h], CHUNKS[h]), pl.ds(k * TILE, TILE)],
                    cats[h].at[32 * arr + 2 * me + k],
                    own_sem.at[h, arr, k],
                )
                c.start()
                own.append(c)
    wcopies = [
        pltpu.make_async_copy(gw, wg, w_sem.at[0]),
        pltpu.make_async_copy(uw, wu, w_sem.at[1]),
    ] + [
        pltpu.make_async_copy(dw.at[:, pl.ds(1024 * i, 1024)], wd.at[i], w_sem.at[2 + i])
        for i in range(4)
    ]
    for c in wcopies:
        c.start()

    barrier = pltpu.get_barrier_semaphore()
    z_next = [(mod4(cz + d) * 2 + cc, me) for d in (1, -1)]
    near = [
        (dp, mod4(cx + 1) * 4 + cy),
        (dp, mod4(cx - 1) * 4 + cy),
        (dp, cx * 4 + mod4(cy + 1)),
        (dp, cx * 4 + mod4(cy - 1)),
        (cz * 2 + 1 - cc, me),
    ] + z_next
    for dev in near:
        pl.semaphore_signal(barrier, inc=1, device_id=dev, device_id_type=MESH)
    pl.semaphore_wait(barrier, len(near))

    def rcopy(src, dst, ssem, rsem, dev):
        return pltpu.make_async_remote_copy(
            src_ref=src, dst_ref=dst, send_sem=ssem, recv_sem=rsem, device_id=dev, device_id_type=MESH
        )

    def send(src, dst, ssem, rsem, dev):
        c = rcopy(src, dst, ssem, rsem, dev)
        c.start()
        sends.append(c)

    outs = []

    def put_out(src, dst, idx):
        c = pltpu.make_async_copy(src, dst, o_sem.at[idx])
        c.start()
        outs.append(c)

    def tensor_at(first_is_x, a1, a2):
        return a1 * 4 + a2 if first_is_x else a2 * 4 + a1

    def ag(h, arr):
        R = CHUNKS[h]
        fx = arr == 0
        c1, c2 = (cx, cy) if fx else (cy, cx)

        def dev(d1, d2):
            return (dp, tensor_at(fx, mod4(c1 + d1), mod4(c2 + d2)))

        def region(d1, d2, part):
            t = tensor_at(fx, mod4(c1 + d1), mod4(c2 + d2))
            rows = (pl.ds(0, R), pl.ds(0, R // 2), pl.ds(R // 2, R // 2))[part]
            return cats[h].at[pl.ds(32 * arr + 2 * t, 2), rows, :]

        def put(idx, d1, d2, part, e1, e2):
            r = region(d1, d2, part)
            send(r, r, ag_s.at[h, arr, idx], ag_r.at[h, arr, idx], dev(e1, e2))

        def got(idx, d1, d2, part):
            r = region(d1, d2, part)
            rcopy(r, r, ag_s.at[h, arr, idx], ag_r.at[h, arr, idx], dev(1, 0)).wait_recv()

        def start():
            put(0, 0, 0, 0, 1, 0)
            put(1, 0, 0, 0, -1, 0)
            put(4, 0, 0, 0, 0, 1)
            put(5, 0, 0, 0, 0, -1)

        def spread(j):
            put(4 + 4 * j, OFF[j], 0, 0, 0, 1)
            put(5 + 4 * j, OFF[j], 0, 0, 0, -1)

        def e1():
            got(0, -1, 0, 0)
            put(2, -1, 0, 1, 1, 0)
            spread(1)

        def e2():
            got(1, 1, 0, 0)
            put(3, 1, 0, 2, -1, 0)
            spread(2)

        def e3():
            got(2, 2, 0, 1)
            got(3, 2, 0, 2)
            spread(3)

        def e4(j):
            got(4 + 4 * j, OFF[j], -1, 0)
            put(6 + 4 * j, OFF[j], -1, 1, 0, 1)
            got(5 + 4 * j, OFF[j], 1, 0)
            put(7 + 4 * j, OFF[j], 1, 2, 0, -1)

        def e5(j):
            got(6 + 4 * j, OFF[j], 2, 1)
            got(7 + 4 * j, OFF[j], 2, 2)

        return start, e1, e2, e3, e4, e5

    AG = [[ag(h, arr) for arr in range(2)] for h in range(NC)]

    def ag_step(h, k, *a):
        for arr in range(2):
            AG[h][arr][k](*a)

    def fwd(h, off, n):
        cat, rr = cats[h], pl.ds(0, CHUNKS[h])
        yy, xx = mod4(cy + off), mod4(cx + off)
        cols = pl.ds(n * 256, 256)

        def total(acc, v):
            for k in range(2):
                vk = v[:, k * TILE : (k + 1) * TILE]
                acc[2 * n + k, rr, :] = vk if off == 0 else acc[2 * n + k, rr, :] + vk

        lhs = jnp.concatenate(
            [cat[2 * (4 * i + yy) + k] for i in range(4) for k in range(2)], axis=1
        )
        for w, acc in ((wg, acc_g), (wu, acc_u)):
            rhs = jnp.concatenate([w[4 * i + yy, :, cols] for i in range(4)], axis=0)
            total(acc, jnp.dot(lhs, rhs, preferred_element_type=jnp.float32))
        lhs = jnp.concatenate([cat[GB + 8 * xx + k] for k in range(8)], axis=1)
        total(acc_h, lax.dot_general(lhs, wd[xx, cols, :], NT, preferred_element_type=jnp.float32))

    def pointwise(h):
        cat = cats[h]

        def body(f, _):
            for r in range(CHUNKS[h] // 64):
                rows = pl.ds(r * 64, 64)
                g, u, hg = acc_g[f, rows, :], acc_u[f, rows, :], acc_h[f, rows, :]
                s = 1.0 / (1.0 + jnp.exp(-g))
                gs = g * s
                cat[HB + f, rows, :] = (gs * u).astype(jnp.bfloat16)
                cat[GGB + f, rows, :] = (hg * u * s * (1.0 + g * (1.0 - s))).astype(jnp.bfloat16)
                cat[GUB + f, rows, :] = (hg * gs).astype(jnp.bfloat16)
            return 0

        lax.fori_loop(0, 6, body, 0)

    def partial(h, off, half):
        cat = cats[h]
        yy = mod4(cy + off)
        at = [4 * i + yy for i in (2 * half, 2 * half + 1)]
        lhs = jnp.concatenate(
            [jnp.concatenate([wg[t], wu[t]], axis=1) for t in at], axis=0
        )
        rhs = jnp.concatenate([cat[GGB + k] for k in range(12)], axis=1)
        v = lax.dot_general(lhs, rhs, NT, preferred_element_type=jnp.float32)
        v = v.astype(jnp.bfloat16)
        for i, t in enumerate(at):
            ps[h][t] = v[256 * i : 256 * (i + 1)]

    def rs(h, p):
        fx = p == 1
        c1, c2 = (cx, cy) if fx else (cy, cx)
        buf = ps[h]
        r0 = p * 128
        full, low, up = pl.ds(r0, 128), pl.ds(r0, 64), pl.ds(r0 + 64, 64)

        def dev(d1, d2):
            return (dp, tensor_at(fx, mod4(c1 + d1), mod4(c2 + d2)))

        def blk(d1, d2):
            return tensor_at(fx, mod4(c1 + d1), mod4(c2 + d2))

        def put(idx, d1, d2, rows, dst, e1, e2):
            send(buf.at[blk(d1, d2), rows, :], dst, rs_s.at[h, p, idx], rs_r.at[h, p, idx], dev(e1, e2))

        def got(idx, dst):
            rcopy(dst, dst, rs_s.at[h, p, idx], rs_r.at[h, p, idx], dev(1, 0)).wait_recv()

        def add(d1, d2, rows, *terms):
            b = blk(d1, d2)
            v = buf[b, rows, :].astype(jnp.float32)
            for ref in terms:
                v = v + ref[...].astype(jnp.float32)
            return b, v

        def addto(d1, d2, rows, *terms):
            b, v = add(d1, d2, rows, *terms)
            buf[b, rows, :] = v.astype(jnp.bfloat16)

        R1 = [[r1[h].at[p, j, k] for k in range(2)] for j in range(4)]
        R2 = [[r2[h].at[p, j, k] for k in range(2)] for j in range(4)]
        R3 = [r3[h].at[p, k] for k in range(2)]
        R4 = [r4[h].at[p, k] for k in range(2)]

        def s1(j):
            put(4 * j, 2, OFF2[j], low, R1[j][0], 1, 0)
            put(4 * j + 1, 2, OFF2[j], up, R1[j][1], -1, 0)

        def t1(j):
            got(4 * j, R1[j][0])
            addto(1, OFF2[j], low, R1[j][0])
            put(4 * j + 2, 1, OFF2[j], full, R2[j][0], 1, 0)
            got(4 * j + 1, R1[j][1])
            addto(-1, OFF2[j], up, R1[j][1])
            put(4 * j + 3, -1, OFF2[j], full, R2[j][1], -1, 0)

        def t2(j):
            got(4 * j + 2, R2[j][0])
            got(4 * j + 3, R2[j][1])
            addto(0, OFF2[j], full, R2[j][0], R2[j][1])
            if j == 0:
                put(16, 0, 2, low, R3[0], 0, 1)
                put(17, 0, 2, up, R3[1], 0, -1)

        def t3():
            got(16, R3[0])
            addto(0, 1, low, R3[0])
            put(18, 0, 1, full, R4[0], 0, 1)
            got(17, R3[1])
            addto(0, -1, up, R3[1])
            put(19, 0, -1, full, R4[1], 0, -1)

        def t4():
            got(18, R4[0])
            got(19, R4[1])
            _, v = add(0, 0, full, R4[0], R4[1])
            rows, cols = pl.ds(STARTS[h], CHUNKS[h]), pl.ds(r0, 128)
            ox[rows, cols] = v.T.astype(jnp.bfloat16)
            put_out(ox.at[rows, cols], out_x.at[rows, cols], 2 * h + p)

        return s1, t1, t2, t3, t4

    RS = [[rs(h, p) for p in range(2)] for h in range(NC)]

    def rs_step(h, k, *a):
        for p in range(2):
            RS[h][p][k](*a)

    UN = 4

    squares = {}

    def tiles_of(h, q0, q1):
        cat, ne = cats[h], NSEQ[h]

        def body(q, carry):
            sq = list(carry)
            for i in range(UN):
                s = q * UN + i
                f, m, kd = sf[s], sm[s], sk[s]
                live = jnp.where(s < lc[0], 1.0, 0.0).astype(jnp.float32)
                li = jnp.where(kd == 2, HB + f, XB + m)
                ri = jnp.where(kd == 0, GGB + f, jnp.where(kd == 1, GUB + f, GB + m))
                for e in range(ne):
                    rows = pl.ds(e * LEN, LEN)
                    v = lax.dot_general(
                        cat[li, rows, :], cat[ri, rows, :], TN, preferred_element_type=jnp.float32
                    )
                    v = v * live
                    tiles[SEQ0[h] + e, s] = v
                    sq[e] = sq[e] + jnp.sum((v * v).reshape(16, 8, TILE), axis=0)
            return tuple(sq)

        z = jnp.zeros((8, TILE), jnp.float32)
        sq = lax.fori_loop(q0, q1, body, squares.pop(h, (z,) * ne))
        if q1 < SLOTS // UN:
            squares[h] = sq
            return
        for e in range(ne):
            nr[h, me, pl.ds(e, 1), :] = jnp.sum(sq[e], axis=0, keepdims=True)

    def norm_send(h):
        for k in range(1, 16):
            r = nr.at[h, me]
            send(r, r, nr_s.at[h, k], nr_r.at[h, k], (dp, lax.rem(me + k, 16)))

    def norm_wait(h):
        for k in range(1, 16):
            src = nr.at[h, lax.rem(me + 16 - k, 16)]
            rcopy(src, src, nr_s.at[h, k], nr_r.at[h, k], (dp, lax.rem(me + k, 16))).wait_recv()
        tot = nr[h, 0]
        for k in range(1, 16):
            tot = tot + nr[h, k]
        tot = jnp.sum(tot, axis=1, keepdims=True)
        clip = jnp.minimum(1.0, BOUND / jnp.sqrt(tot + 1e-06))
        clip = jnp.broadcast_to(clip, (8, TILE))
        return [clip[e : e + 1, :] for e in range(NSEQ[h])]

    def fold(cl):
        def body(s, _):
            v = cl[0] * tiles[0, s]
            for e in range(1, len(cl)):
                v = v + cl[e] * tiles[e, s]
            tiles[0, s] = v
            return 0

        lax.fori_loop(0, SLOTS, body, 0)

    partner = (cz * 2 + 1 - cc, me)
    terms = [0] + [SEQ0[-1] + e for e in range(NSEQ[-1])]

    def rows_of(z, c):
        return pl.ds(pl.multiple_of((2 * z + c) * 16, 16), 16)

    def to_partner(k):
        def body(s, _):
            for z in range(4):
                xs[k, z, s] = tiles[terms[k], s, rows_of(z, 1 - cc), :].astype(jnp.bfloat16)
            return 0

        lax.fori_loop(0, SLOTS, body, 0)
        send(xs.at[k], xr.at[k], x_s.at[k], x_r.at[k], partner)

    def clip_to_partner(cl):
        for e in range(NSEQ[-1]):
            cs[pl.ds(e, 1), :] = cl[e]
        send(cs, cr, c_s.at[0], c_r.at[0], partner)

    def partner_clip():
        rcopy(cr, cr, c_s.at[0], c_r.at[0], partner).wait_recv()
        return [cr[pl.ds(e, 1), :] for e in range(NSEQ[-1])]

    def from_partner(k):
        rcopy(xr.at[k], xr.at[k], x_s.at[k], x_r.at[k], partner).wait_recv()

    def combined(z, s, cl, pcl):
        v = tiles[0, s, rows_of(z, cc), :] + xr[0, z, s].astype(jnp.float32)
        for e in range(NSEQ[-1]):
            v = v + cl[e] * tiles[terms[e + 1], s, rows_of(z, cc), :]
            v = v + pcl[e] * xr[e + 1, z, s].astype(jnp.float32)
        return v

    HALF = (pl.ds(0, SLOTS // 2), pl.ds(SLOTS // 2, SLOTS // 2))

    def combine(d, half, cl, pcl):
        z = mod4(cz + d)

        def body(i, _):
            s = half * (SLOTS // 2) + i
            zs[z, s] = combined(z, s, cl, pcl).astype(jnp.bfloat16)
            return 0

        lax.fori_loop(0, SLOTS // 2, body, 0)

    def zput(idx, d_block, half, dst, d):
        send(
            zs.at[mod4(cz + d_block), HALF[half]],
            zr.at[dst, HALF[half]],
            z_s.at[idx],
            z_r.at[idx],
            (mod4(cz + d) * 2 + cc, me),
        )

    def zgot(idx, dst, half):
        r = zr.at[dst, HALF[half]]
        rcopy(r, r, z_s.at[idx], z_r.at[idx], (mod4(cz + 1) * 2 + cc, me)).wait_recv()

    def zadd(d_block, half, src):
        z = mod4(cz + d_block)
        v = zs[z, HALF[half]].astype(jnp.float32) + zr[src, HALF[half]].astype(jnp.float32)
        zs[z, HALF[half]] = v.astype(jnp.bfloat16)

    def z_start(cl, pcl):
        combine(2, 0, cl, pcl)
        zput(0, 2, 0, 0, 1)
        combine(2, 1, cl, pcl)
        zput(1, 2, 1, 1, -1)
        combine(1, 1, cl, pcl)
        zput(2, 1, 1, 2, 1)
        combine(-1, 0, cl, pcl)
        zput(3, -1, 0, 3, -1)
        combine(1, 0, cl, pcl)
        combine(-1, 1, cl, pcl)

    def z_pass():
        zgot(0, 0, 0)
        zadd(1, 0, 0)
        zput(4, 1, 0, 2, 1)
        zgot(1, 1, 1)
        zadd(-1, 1, 1)
        zput(5, -1, 1, 3, -1)

    def z_own(cl, pcl):
        def body(s, _):
            ob[s] = combined(cz, s, cl, pcl)
            return 0

        lax.fori_loop(0, SLOTS, body, 0)

    def z_end(half):
        zgot(2 if half else 4, 2, half)
        zgot(5 if half else 3, 3, half)
        sl = HALF[half]
        ob[sl] = ob[sl] + zr[2, sl].astype(jnp.float32) + zr[3, sl].astype(jnp.float32)
        put_out(ob.at[sl], out_b.at[sl], 2 * NC + half)

    J = range(4)
    N = range(3)
    for c in own[:4]:
        c.wait()
    ag_step(0, 0)
    for c in own[4:]:
        c.wait()
    nr[:, me] = jnp.zeros((NC, 8, TILE), jnp.float32)
    cs[...] = jnp.zeros((8, TILE), jnp.float32)
    ag_step(0, 1)
    ag_step(0, 2)
    ag_step(1, 0)
    ag_step(0, 3)
    for c in wcopies:
        c.wait()
    ag_step(0, 4, 0)
    for n in N:
        fwd(0, 0, n)
        ag_step(0, 4, n + 1)
    ag_step(1, 1)
    fwd(0, -1, 0)
    ag_step(1, 2)
    fwd(0, -1, 1)
    ag_step(0, 5, 0)
    fwd(0, -1, 2)
    ag_step(1, 3)
    for n in N:
        fwd(0, 1, n)
        ag_step(0, 5, n + 1)
    for n in N:
        fwd(0, 2, n)
    ag_step(1, 4, 0)
    pointwise(0)
    for k in J:
        partial(0, OFF2[k], 0)
        partial(0, OFF2[k], 1)
        if k == 1:
            ag_step(1, 4, 1)
    tiles_of(0, 0, 6)
    ag_step(1, 4, 2)
    tiles_of(0, 6, 12)
    norm_send(0)
    ag_step(1, 4, 3)
    for k in J:
        rs_step(0, 0, k)
    for n in N:
        fwd(1, 0, n)
    for n in N:
        fwd(1, -1, n)
    for j in J:
        rs_step(0, 1, j)
    for n in N:
        fwd(1, 1, n)
    for j in J:
        ag_step(1, 5, j)
    for n in N:
        fwd(1, 2, n)
    pointwise(1)
    tiles_of(1, 0, 6)
    rs_step(0, 2, 0)
    rs_step(0, 2, 1)
    tiles_of(1, 6, 12)
    norm_send(1)
    for k in range(1, NT1):
        to_partner(k)
    rs_step(0, 2, 2)
    rs_step(0, 2, 3)
    rs_step(0, 3)
    fold(norm_wait(0))
    to_partner(0)
    partial(1, 2, 0)
    partial(1, 2, 1)
    for k in J:
        RS[1][0][0](k)
    RS[1][1][0](0)
    partial(1, 1, 0)
    partial(1, 1, 1)
    RS[1][1][0](1)
    clip = norm_wait(1)
    clip_to_partner(clip)
    for k in (2, 3):
        partial(1, OFF2[k], 0)
        partial(1, OFF2[k], 1)
        RS[1][1][0](k)
    for k in range(NT1):
        from_partner(k)
    pclip = partner_clip()
    z_start(clip, pclip)
    for j in J:
        rs_step(1, 1, j)
    rs_step(0, 4)
    z_pass()
    z_own(clip, pclip)
    for j in J:
        rs_step(1, 2, j)
    rs_step(1, 3)
    z_end(1)
    z_end(0)
    rs_step(1, 4)
    for c in sends:
        c.wait_send()
    for c in outs:
        c.wait()


def hand_out(x, b, out_x, out_b, vx, vb, sem):
    ins = [pltpu.make_async_copy(x, vx, sem.at[0]), pltpu.make_async_copy(b, vb, sem.at[1])]
    outs = [pltpu.make_async_copy(vx, out_x, sem.at[2]), pltpu.make_async_copy(vb, out_b, sem.at[3])]
    for c in ins:
        c.start()
    for i, o in zip(ins, outs):
        i.wait()
        o.start()
    for o in outs:
        o.wait()


def per_device(
    tokens,
    out_grad,
    gate_weight,
    up_weight,
    down_weight,
    slot_ffn_block,
    slot_model_block,
    slot_kind,
    live_count,
):
    bf, f32 = jnp.bfloat16, jnp.float32
    anyspec = pl.BlockSpec(memory_space=pl.ANY)
    smem = pl.BlockSpec(memory_space=pltpu.SMEM)
    dma = pltpu.SemaphoreType.DMA
    grad_x, grad_b = pl.pallas_call(
        kernel,
        out_shape=(
            jax.ShapeDtypeStruct((512, 256), bf),
            jax.ShapeDtypeStruct((SLOTS, 16, TILE), f32),
        ),
        in_specs=[anyspec] * 5 + [smem] * 4,
        out_specs=(anyspec, anyspec),
        scratch_shapes=[
            [pltpu.VMEM((BLOCKS, r, TILE), bf) for r in CHUNKS],
            pltpu.VMEM((16, 256, 768), bf),
            pltpu.VMEM((16, 256, 768), bf),
            pltpu.VMEM((4, 768, 1024), bf),
            pltpu.VMEM((6, max(CHUNKS), TILE), f32),
            pltpu.VMEM((6, max(CHUNKS), TILE), f32),
            pltpu.VMEM((6, max(CHUNKS), TILE), f32),
            [pltpu.VMEM((16, 256, r), bf) for r in CHUNKS],
            [pltpu.VMEM((2, 4, 2, 64, r), bf) for r in CHUNKS],
            [pltpu.VMEM((2, 4, 2, 128, r), bf) for r in CHUNKS],
            [pltpu.VMEM((2, 2, 64, r), bf) for r in CHUNKS],
            [pltpu.VMEM((2, 2, 128, r), bf) for r in CHUNKS],
            pltpu.VMEM((4, SLOTS, TILE, TILE), f32),
            pltpu.VMEM((NC, 16, 8, TILE), f32),
            pltpu.VMEM((NT1, 4, SLOTS, 16, TILE), bf),
            pltpu.VMEM((NT1, 4, SLOTS, 16, TILE), bf),
            pltpu.VMEM((8, TILE), f32),
            pltpu.VMEM((8, TILE), f32),
            pltpu.VMEM((4, SLOTS, 16, TILE), bf),
            pltpu.VMEM((4, SLOTS, 16, TILE), bf),
            dma((NC, 2, 2)),
            dma((6,)),
            dma((NC, 2, 20)),
            dma((NC, 2, 20)),
            dma((NC, 2, 20)),
            dma((NC, 2, 20)),
            dma((NC, 16)),
            dma((NC, 16)),
            dma((NT1,)),
            dma((NT1,)),
            dma((1,)),
            dma((1,)),
            dma((6,)),
            dma((6,)),
            dma((2 * NC + 2,)),
            pltpu.VMEM((512, 256), bf),
            pltpu.VMEM((SLOTS, 16, TILE), f32),
        ],
        compiler_params=pltpu.CompilerParams(
            collective_id=0, has_side_effects=True, vmem_limit_bytes=62 << 20
        ),
        cost_estimate=pl.CostEstimate(
            flops=17_000_000_000, bytes_accessed=20_000_000, transcendentals=400_000
        ),
    )(
        tokens,
        out_grad,
        gate_weight.reshape(16, 256, 768),
        up_weight.reshape(16, 256, 768),
        down_weight,
        slot_ffn_block,
        slot_model_block,
        slot_kind,
        live_count,
    )
    return pl.pallas_call(
        hand_out,
        out_shape=(
            jax.ShapeDtypeStruct((512, 256), bf),
            jax.ShapeDtypeStruct((SLOTS, 16, TILE), f32),
        ),
        in_specs=[anyspec] * 2,
        out_specs=(anyspec, anyspec),
        scratch_shapes=[
            pltpu.VMEM((512, 256), bf),
            pltpu.VMEM((SLOTS, 16, TILE), f32),
            dma((4,)),
        ],
    )(grad_x, grad_b)


def solution(mesh):
    return jax.shard_map(
        per_device,
        mesh=mesh,
        in_specs=(
            P("dp", "tensor"),
            P("dp", "tensor"),
            P(None, "tensor"),
            P(None, "tensor"),
            P("tensor", None),
            P("tensor"),
            P("tensor"),
            P("tensor"),
            P("tensor"),
        ),
        out_specs=(P("dp", "tensor"), P("tensor", "dp", None)),
        check_vma=False,
    )
```

time: 105 us -> 100 us (0.952); the launches traced: 103 us -> 99.8 us
  local copies, waits for them, and re-layouts: 3.44 us -> 0 us
    unnamed x2 -> x0, local copies, waits for them, and re-layouts: 3.44 us -> none
    pallas_call x1, Pallas kernels: 98.7 us -> 96.5 us  [per_device(): pl.pallas_call(kernel, out_shape=(jax.ShapeDtypeStruct((512, 256), bf), j...]
    pallas_call x0 -> x1, Pallas kernels: none -> 1.86 us  [per_device(): pl.pallas_call(hand_out, out_shape=(jax.ShapeDtypeStruct((512, 256), bf),...]
where the time goes in v2:
time: 100 us; the launch traced here: 99.8 us
  Pallas kernels  98.4 us (98%)
  between operations  1.45 us (1%)
    pallas_call x1, Pallas kernels, per_device(): pl.pallas_call(kernel, out_shape=(jax.ShapeDtypeStruct((512, 256), bf), j...  96.5 us

profile of v2, /device:TPU:0, one launch (start us, length us, event | category | flops | bytes accessed | tf_op | source)
XLA Modules:
  0.0 99.8 jit_solution(5194051768116083648)
XLA Ops:
  1.3 96.5 %shard_map.104 = (bf16[512,256]{1,0:T(8,128)(2,1)}, f32[48,16,128]{2,1,0:T(8,128)}) custom-call(bf16[512,256]{1,0:T(8,128)(2,1)} %tok.1, bf16[512,256]{1,0:T(8,128)(2,1)} %og.1, bf16[16,256,768]{2,1,0:T(8,128)(2,1)} %bitcast.2, bf16[16,256,768]{2,1,0:T(8,128)(2,1)} %bitcast.3, bf16[768,4096]{1,0:T(8,128)(2,1)} %dw.1, s32[48]{0:T(128)} %sf.1, s32[48]{0:T(128)} %sm.1, ...), custom_call_target="tpu_custom_call" | custom-call | flops 16999999488 | bytes 20000000 | tf_op jit(solution)/shard_map/pallas_call | solution.py:625
  97.8 1.9 %shard_map.105 = (bf16[512,256]{1,0:T(8,128)(2,1)}, f32[48,16,128]{2,1,0:T(8,128)}) custom-call(bf16[512,256]{1,0:T(8,128)(2,1)} %get-tuple-element.4.x, f32[48,16,128]{2,1,0:T(8,128)} %get-tuple-element.5.b), custom_call_target="tpu_custom_call" | custom-call | tf_op jit(solution)/shard_map/pallas_call | solution.py:689

commit v3 on v2

--- a/solution.py
+++ b/solution.py
@@ -490,105 +490,181 @@
         ob[sl] = ob[sl] + zr[2, sl].astype(jnp.float32) + zr[3, sl].astype(jnp.float32)
         put_out(ob.at[sl], out_b.at[sl], 2 * NC + half)
 
-    J = range(4)
-    N = range(3)
     for c in own[:4]:
         c.wait()
-    ag_step(0, 0)
+    AG[0][0][0]()
+    AG[0][1][0]()
     for c in own[4:]:
         c.wait()
     nr[:, me] = jnp.zeros((NC, 8, TILE), jnp.float32)
     cs[...] = jnp.zeros((8, TILE), jnp.float32)
-    ag_step(0, 1)
-    ag_step(0, 2)
-    ag_step(1, 0)
-    ag_step(0, 3)
+    AG[0][0][2]()
+    AG[0][0][1]()
+    AG[0][1][1]()
+    AG[0][1][2]()
+    AG[0][0][3]()
+    AG[0][0][4](0)
+    AG[0][0][4](2)
+    AG[0][1][4](0)
     for c in wcopies:
         c.wait()
-    ag_step(0, 4, 0)
-    for n in N:
-        fwd(0, 0, n)
-        ag_step(0, 4, n + 1)
-    ag_step(1, 1)
+    AG[0][1][4](1)
+    AG[0][1][3]()
+    AG[0][0][4](3)
+    AG[0][1][4](2)
+    fwd(0, 0, 2)
+    AG[0][0][4](1)
+    fwd(0, 0, 0)
+    AG[1][0][0]()
+    AG[0][1][5](0)
+    AG[0][0][5](2)
+    AG[0][1][4](3)
+    fwd(0, 0, 1)
+    AG[1][1][0]()
+    fwd(0, 1, 0)
+    fwd(0, 1, 2)
+    fwd(0, 1, 1)
+    AG[0][0][5](3)
+    fwd(0, -1, 2)
+    AG[0][0][5](0)
+    AG[0][0][5](1)
+    fwd(0, -1, 1)
+    AG[1][0][1]()
     fwd(0, -1, 0)
-    ag_step(1, 2)
-    fwd(0, -1, 1)
-    ag_step(0, 5, 0)
-    fwd(0, -1, 2)
-    ag_step(1, 3)
-    for n in N:
-        fwd(0, 1, n)
-        ag_step(0, 5, n + 1)
-    for n in N:
-        fwd(0, 2, n)
-    ag_step(1, 4, 0)
+    AG[0][1][5](2)
+    AG[0][1][5](3)
+    AG[0][1][5](1)
+    fwd(0, 2, 0)
+    AG[1][0][2]()
+    fwd(0, 2, 1)
+    fwd(0, 2, 2)
+    AG[1][1][1]()
     pointwise(0)
-    for k in J:
-        partial(0, OFF2[k], 0)
-        partial(0, OFF2[k], 1)
-        if k == 1:
-            ag_step(1, 4, 1)
     tiles_of(0, 0, 6)
-    ag_step(1, 4, 2)
+    AG[1][1][2]()
+    AG[1][1][4](0)
     tiles_of(0, 6, 12)
+    AG[1][0][3]()
     norm_send(0)
-    ag_step(1, 4, 3)
-    for k in J:
-        rs_step(0, 0, k)
-    for n in N:
-        fwd(1, 0, n)
-    for n in N:
-        fwd(1, -1, n)
-    for j in J:
-        rs_step(0, 1, j)
-    for n in N:
-        fwd(1, 1, n)
-    for j in J:
-        ag_step(1, 5, j)
-    for n in N:
-        fwd(1, 2, n)
+    partial(0, OFF2[0], 0)
+    partial(0, OFF2[0], 1)
+    RS[0][0][0](0)
+    partial(0, OFF2[1], 0)
+    partial(0, OFF2[1], 1)
+    RS[0][1][0](0)
+    RS[0][0][0](3)
+    partial(0, OFF2[2], 0)
+    partial(0, OFF2[2], 1)
+    AG[1][0][4](0)
+    AG[1][1][3]()
+    partial(0, OFF2[3], 0)
+    partial(0, OFF2[3], 1)
+    AG[1][0][4](2)
+    fwd(1, 0, 0)
+    fwd(1, 0, 1)
+    AG[1][0][4](1)
+    AG[1][0][4](3)
+    early = norm_wait(0)
+    AG[1][1][4](2)
+    AG[1][1][4](1)
+    RS[0][0][1](0)
+    fold(early)
+    RS[0][0][0](1)
+    RS[0][0][1](3)
+    fwd(1, 0, 2)
+    AG[1][1][4](3)
+    fwd(1, 1, 2)
+    AG[1][1][5](0)
+    fwd(1, 1, 1)
+    fwd(1, -1, 2)
+    fwd(1, -1, 1)
+    fwd(1, -1, 0)
+    RS[0][1][0](1)
+    AG[1][0][5](0)
+    AG[1][1][5](1)
+    RS[0][1][0](3)
+    RS[0][0][0](2)
+    RS[0][1][0](2)
+    RS[0][1][1](0)
+    fwd(1, 1, 0)
+    AG[1][0][5](1)
+    AG[1][0][5](2)
+    AG[1][1][5](2)
+    AG[1][0][5](3)
+    AG[1][1][5](3)
+    fwd(1, 2, 1)
+    fwd(1, 2, 2)
+    fwd(1, 2, 0)
     pointwise(1)
+    partial(1, OFF2[0], 0)
+    partial(1, OFF2[0], 1)
+    partial(1, OFF2[1], 0)
+    partial(1, OFF2[1], 1)
+    RS[1][0][0](0)
+    RS[1][1][0](0)
+    RS[1][0][0](1)
+    RS[0][1][1](2)
+    RS[1][1][0](1)
     tiles_of(1, 0, 6)
-    rs_step(0, 2, 0)
-    rs_step(0, 2, 1)
+    RS[0][1][1](1)
+    RS[0][1][1](3)
+    RS[1][0][0](2)
     tiles_of(1, 6, 12)
     norm_send(1)
-    for k in range(1, NT1):
-        to_partner(k)
-    rs_step(0, 2, 2)
-    rs_step(0, 2, 3)
-    rs_step(0, 3)
-    fold(norm_wait(0))
+    RS[1][0][0](3)
+    RS[0][0][1](1)
+    RS[1][1][1](0)
+    partial(1, OFF2[2], 0)
+    partial(1, OFF2[2], 1)
+    RS[1][0][1](0)
+    RS[1][1][0](2)
+    RS[0][0][1](2)
+    to_partner(1)
+    partial(1, OFF2[3], 0)
+    partial(1, OFF2[3], 1)
+    RS[1][1][0](3)
+    to_partner(2)
+    RS[0][0][2](0)
     to_partner(0)
-    partial(1, 2, 0)
-    partial(1, 2, 1)
-    for k in J:
-        RS[1][0][0](k)
-    RS[1][1][0](0)
-    partial(1, 1, 0)
-    partial(1, 1, 1)
-    RS[1][1][0](1)
+    RS[1][1][1](1)
+    RS[1][0][1](1)
     clip = norm_wait(1)
     clip_to_partner(clip)
-    for k in (2, 3):
-        partial(1, OFF2[k], 0)
-        partial(1, OFF2[k], 1)
-        RS[1][1][0](k)
+    RS[1][0][1](2)
+    RS[1][1][1](2)
+    RS[1][0][2](0)
+    RS[1][1][2](0)
+    RS[0][1][2](0)
+    RS[1][1][1](3)
     for k in range(NT1):
         from_partner(k)
     pclip = partner_clip()
     z_start(clip, pclip)
-    for j in J:
-        rs_step(1, 1, j)
-    rs_step(0, 4)
+    RS[1][0][1](3)
+    RS[0][0][2](2)
+    RS[0][0][2](1)
+    RS[0][0][3]()
+    RS[0][1][2](1)
+    RS[1][1][2](2)
+    RS[1][1][2](1)
+    RS[1][0][2](2)
+    RS[1][1][3]()
+    RS[1][0][2](1)
+    RS[0][1][2](2)
+    RS[1][0][3]()
+    RS[0][1][3]()
     z_pass()
     z_own(clip, pclip)
-    for j in J:
-        rs_step(1, 2, j)
-    rs_step(1, 3)
+    RS[1][0][2](3)
+    RS[1][1][2](3)
+    RS[0][0][2](3)
+    RS[0][1][2](3)
+    RS[0][0][4]()
+    RS[1][0][4]()
+    RS[1][1][4]()
+    RS[0][1][4]()
+    z_end(0)
     z_end(1)
-    z_end(0)
-    rs_step(1, 4)
     for c in sends:
         c.wait_send()
     for c in outs:

time: 100 us -> 90.5 us (0.905)
  Pallas kernels: 98.4 us -> 88.9 us
    pallas_call x1, Pallas kernels: 96.5 us -> 87 us  [per_device(): pl.pallas_call(kernel, out_shape=(jax.ShapeDtypeStruct((512, 256), bf), j...]
where the time goes in v3:
time: 90.5 us; the launch traced here: 90.3 us
  Pallas kernels  88.9 us (98%)
  between operations  1.45 us (2%)
    pallas_call x1, Pallas kernels, per_device(): pl.pallas_call(kernel, out_shape=(jax.ShapeDtypeStruct((512, 256), bf), j...  87 us
    pallas_call x1, Pallas kernels, per_device(): pl.pallas_call(hand_out, out_shape=(jax.ShapeDtypeStruct((512, 256), bf),...  1.86 us

profile of v3, /device:TPU:0, one launch (start us, length us, event | category | flops | bytes accessed | tf_op | source)
XLA Modules:
  0.0 90.3 jit_solution(7461000724271133656)
XLA Ops:
  1.3 87.0 %shard_map.104 = (bf16[512,256]{1,0:T(8,128)(2,1)}, f32[48,16,128]{2,1,0:T(8,128)}) custom-call(bf16[512,256]{1,0:T(8,128)(2,1)} %tok.1, bf16[512,256]{1,0:T(8,128)(2,1)} %og.1, bf16[16,256,768]{2,1,0:T(8,128)(2,1)} %bitcast.2, bf16[16,256,768]{2,1,0:T(8,128)(2,1)} %bitcast.3, bf16[768,4096]{1,0:T(8,128)(2,1)} %dw.1, s32[48]{0:T(128)} %sf.1, s32[48]{0:T(128)} %sm.1, ...), custom_call_target="tpu_custom_call" | custom-call | flops 16999999488 | bytes 20000000 | tf_op jit(solution)/shard_map/pallas_call | solution.py:701
  88.3 1.9 %shard_map.105 = (bf16[512,256]{1,0:T(8,128)(2,1)}, f32[48,16,128]{2,1,0:T(8,128)}) custom-call(bf16[512,256]{1,0:T(8,128)(2,1)} %get-tuple-element.4.x, f32[48,16,128]{2,1,0:T(8,128)} %get-tuple-element.5.b), custom_call_target="tpu_custom_call" | custom-call | tf_op jit(solution)/shard_map/pallas_call | solution.py:765

commit v4 on v3

--- a/solution.py
+++ b/solution.py
@@ -87,6 +87,18 @@
     cz, cc = dp // 2, lax.rem(dp, 2)
     sends = []
 
+    barrier = pltpu.get_barrier_semaphore()
+    z_next = [(mod4(cz + d) * 2 + cc, me) for d in (1, -1)]
+    near = [
+        (dp, mod4(cx + 1) * 4 + cy),
+        (dp, mod4(cx - 1) * 4 + cy),
+        (dp, cx * 4 + mod4(cy + 1)),
+        (dp, cx * 4 + mod4(cy - 1)),
+        (cz * 2 + 1 - cc, me),
+    ] + z_next
+    for dev in near:
+        pl.semaphore_signal(barrier, inc=1, device_id=dev, device_id_type=MESH)
+
     own = []
     for h in range(NC):
         for arr, src in ((0, tok), (1, og)):
@@ -108,17 +120,6 @@
     for c in wcopies:
         c.start()
 
-    barrier = pltpu.get_barrier_semaphore()
-    z_next = [(mod4(cz + d) * 2 + cc, me) for d in (1, -1)]
-    near = [
-        (dp, mod4(cx + 1) * 4 + cy),
-        (dp, mod4(cx - 1) * 4 + cy),
-        (dp, cx * 4 + mod4(cy + 1)),
-        (dp, cx * 4 + mod4(cy - 1)),
-        (cz * 2 + 1 - cc, me),
-    ] + z_next
-    for dev in near:
-        pl.semaphore_signal(barrier, inc=1, device_id=dev, device_id_type=MESH)
     pl.semaphore_wait(barrier, len(near))
 
     def rcopy(src, dst, ssem, rsem, dev):
@@ -399,12 +400,14 @@
         return pl.ds(pl.multiple_of((2 * z + c) * 16, 16), 16)
 
     def to_partner(k):
-        def body(s, _):
-            for z in range(4):
-                xs[k, z, s] = tiles[terms[k], s, rows_of(z, 1 - cc), :].astype(jnp.bfloat16)
+        def body(q, _):
+            for i in range(UN):
+                s = q * UN + i
+                for z in range(4):
+                    xs[k, z, s] = tiles[terms[k], s, rows_of(z, 1 - cc), :].astype(jnp.bfloat16)
             return 0
 
-        lax.fori_loop(0, SLOTS, body, 0)
+        lax.fori_loop(0, SLOTS // UN, body, 0)
         send(xs.at[k], xr.at[k], x_s.at[k], x_r.at[k], partner)
 
     def clip_to_partner(cl):
@@ -431,12 +434,13 @@
     def combine(d, half, cl, pcl):
         z = mod4(cz + d)
 
-        def body(i, _):
-            s = half * (SLOTS // 2) + i
-            zs[z, s] = combined(z, s, cl, pcl).astype(jnp.bfloat16)
+        def body(q, _):
+            for i in range(UN):
+                s = half * (SLOTS // 2) + q * UN + i
+                zs[z, s] = combined(z, s, cl, pcl).astype(jnp.bfloat16)
             return 0
 
-        lax.fori_loop(0, SLOTS // 2, body, 0)
+        lax.fori_loop(0, SLOTS // 2 // UN, body, 0)
 
     def zput(idx, d_block, half, dst, d):
         send(
@@ -477,11 +481,13 @@
         zput(5, -1, 1, 3, -1)
 
     def z_own(cl, pcl):
-        def body(s, _):
-            ob[s] = combined(cz, s, cl, pcl)
+        def body(q, _):
+            for i in range(UN):
+                s = q * UN + i
+                ob[s] = combined(cz, s, cl, pcl)
             return 0
 
-        lax.fori_loop(0, SLOTS, body, 0)
+        lax.fori_loop(0, SLOTS // UN, body, 0)
 
     def z_end(half):
         zgot(2 if half else 4, 2, half)

time: 90.5 us -> 89.3 us (0.987)
  Pallas kernels: 88.9 us -> 87.3 us
    pallas_call x1, Pallas kernels: 87 us -> 85.4 us  [per_device(): pl.pallas_call(kernel, out_shape=(jax.ShapeDtypeStruct((512, 256), bf), j...]
where the time goes in v4:
time: 89.3 us; the launch traced here: 88.7 us
  Pallas kernels  87.3 us (98%)
  between operations  1.45 us (2%)
    pallas_call x1, Pallas kernels, per_device(): pl.pallas_call(kernel, out_shape=(jax.ShapeDtypeStruct((512, 256), bf), j...  85.4 us
    pallas_call x1, Pallas kernels, per_device(): pl.pallas_call(hand_out, out_shape=(jax.ShapeDtypeStruct((512, 256), bf),...  1.86 us

profile of v4, /device:TPU:0, one launch (start us, length us, event | category | flops | bytes accessed | tf_op | source)
XLA Modules:
  0.0 88.7 jit_solution(9516802908956178295)
XLA Ops:
  1.3 85.4 %shard_map.104 = (bf16[512,256]{1,0:T(8,128)(2,1)}, f32[48,16,128]{2,1,0:T(8,128)}) custom-call(bf16[512,256]{1,0:T(8,128)(2,1)} %tok.1, bf16[512,256]{1,0:T(8,128)(2,1)} %og.1, bf16[16,256,768]{2,1,0:T(8,128)(2,1)} %bitcast.2, bf16[16,256,768]{2,1,0:T(8,128)(2,1)} %bitcast.3, bf16[768,4096]{1,0:T(8,128)(2,1)} %dw.1, s32[48]{0:T(128)} %sf.1, s32[48]{0:T(128)} %sm.1, ...), custom_call_target="tpu_custom_call" | custom-call | flops 16999999488 | bytes 20000000 | tf_op jit(solution)/shard_map/pallas_call | solution.py:707
  86.7 1.9 %shard_map.105 = (bf16[512,256]{1,0:T(8,128)(2,1)}, f32[48,16,128]{2,1,0:T(8,128)}) custom-call(bf16[512,256]{1,0:T(8,128)(2,1)} %get-tuple-element.4.x, f32[48,16,128]{2,1,0:T(8,128)} %get-tuple-element.5.b), custom_call_target="tpu_custom_call" | custom-call | tf_op jit(solution)/shard_map/pallas_call | solution.py:771
